TPU v7x, 512 devices: a whole 4x4x16 slice. The times are simulated.
512 devices in a mesh: wide: 64 (over z_lo, y, core), mid: 4 (over x), narrow: 2 (over z_hi).
Axes of the slice: x: 4, y: 4, z: 16 (z_hi: 2, z_lo: 8; z = z_hi * 8 + z_lo), core: 2. Of those that a mesh axis runs over, the one named last changes fastest.
Arguments:
- amplitudes: float32 [2, 134217728], P(None, ('wide', 'mid', 'narrow')), may hold values from -6 to 6
- gates: float32 [3, 2, 128, 128], replicated, may hold values from -0.375 to 0.375
- qubit_sets: int32 [3, 7], replicated, may hold values from 0 to 17, as said below
Outputs:
- evolved: float32 [2, 134217728], P(None, ('wide', 'mid', 'narrow'))
Inputs may be any that keep to these rules, and one draw needn't show every extreme that they name: `qubit_sets`: in each row the last entry is 17 and the other entries are distinct qubits among 0 to 6.
All inputs are finite; a program needn't handle non-finite values.
Results may differ from a plain program's by a relative error of at most 0.011.
Values may be sent and summed in bfloat16 or wider, within the bound.
A program may use at most 64 MiB of HBM per device.

v0:
```python
import jax
import jax.numpy as jnp
from jax import lax
from jax.sharding import PartitionSpec as P

BLOCK = 256


def from_partner(block, axis, bit):
    count = lax.axis_size(axis)
    route = []
    for low in range(count):
        high = low | 1 << bit
        if high != low and high < count:
            route += [(low, high), (high, low)]
    return lax.ppermute(block, axis, route)


def full_gate(matrix, qubits, local_bits):
    places = jnp.where(qubits == local_bits - 1, 7, qubits)
    spare = 28 - jnp.sum(places)
    cells = jnp.arange(256, dtype=jnp.int32)
    gate_index = jnp.zeros((256,), jnp.int32)
    for bit_pos in range(qubits.shape[0]):
        gate_index = gate_index + ((cells >> places[bit_pos] & 1) << bit_pos)
    select = (gate_index[:, None] == jnp.arange(128, dtype=jnp.int32)[None, :]).astype(jnp.float32)
    spare_bit = cells >> spare & 1
    same = (spare_bit[:, None] == spare_bit[None, :]).astype(jnp.float32)
    spread = jnp.einsum("ak,skj,bj->sab", select, matrix, select, precision=lax.Precision.HIGHEST)
    return spread * same[None]


def encode(outgoing):
    shaped = outgoing.reshape(2, -1, BLOCK)
    magnitude = jnp.max(jnp.abs(shaped), axis=(0, 2)) + 1e-06
    scales = magnitude.astype(jnp.bfloat16)
    mantissas = (shaped / scales.astype(jnp.float32)[None, :, None]).astype(jnp.bfloat16)
    return (mantissas.reshape(2, -1), scales)


def decode(mantissas, scales):
    shaped = mantissas.reshape(2, -1, BLOCK).astype(jnp.float32)
    return (shaped * scales.astype(jnp.float32)[None, :, None]).reshape(2, -1)


def apply_gate(block_in, matrix):
    real_part = jnp.einsum(
        "bk,rk->br", block_in[0], matrix[0], precision=lax.Precision.HIGHEST
    ) - jnp.einsum("bk,rk->br", block_in[1], matrix[1], precision=lax.Precision.HIGHEST)
    imag_part = jnp.einsum(
        "bk,rk->br", block_in[0], matrix[1], precision=lax.Precision.HIGHEST
    ) + jnp.einsum("bk,rk->br", block_in[1], matrix[0], precision=lax.Precision.HIGHEST)
    return jnp.stack([real_part, imag_part])


def run_layer(current, gate_small, qubits, own_bit, transfer):
    half_size = current.shape[1] // 2
    local_bits = current.shape[1].bit_length() - 1
    matrix = full_gate(gate_small, qubits, local_bits)
    lower = current[:, :half_size]
    upper = current[:, half_size:]
    stays_low = own_bit == 0
    outgoing = jnp.where(stays_low, upper, lower)
    resident = jnp.where(stays_low, lower, upper)
    mantissas, scales = encode(outgoing)
    got_mantissas, got_scales = transfer(mantissas, scales)
    incoming = decode(got_mantissas, got_scales)
    new_lower = jnp.where(stays_low, resident, incoming)
    new_upper = jnp.where(stays_low, incoming, resident)
    block_in = jnp.concatenate(
        [new_lower.reshape(2, -1, 128), new_upper.reshape(2, -1, 128)], axis=-1
    )
    result = apply_gate(block_in, matrix)
    return jnp.concatenate(
        [result[:, :, :128].reshape(2, -1), result[:, :, 128:].reshape(2, -1)], axis=1
    )


def on_device(amplitudes, gates, qubit_sets):
    top_bit = lax.axis_size("wide").bit_length() - 2

    def send_high(mantissas, scales):
        return from_partner((mantissas, scales), "wide", top_bit)

    def send_low(mantissas, scales):
        return from_partner((mantissas, scales), "wide", 0)

    def send_narrow(mantissas, scales):
        return from_partner((mantissas, scales), "narrow", 0)

    wide_index = lax.axis_index("wide")
    narrow_index = lax.axis_index("narrow")
    current = run_layer(amplitudes, gates[0], qubit_sets[0], wide_index >> top_bit & 1, send_high)
    current = run_layer(current, gates[1], qubit_sets[1], wide_index & 1, send_low)
    current = run_layer(current, gates[2], qubit_sets[2], narrow_index & 1, send_narrow)
    return current


def solution(mesh):
    in_specs = (P(None, ("wide", "mid", "narrow")), P(), P())
    out_specs = P(None, ("wide", "mid", "narrow"))
    return jax.shard_map(
        on_device, mesh=mesh, in_specs=in_specs, out_specs=out_specs, check_vma=False
    )
```

profile of v0, /device:TPU:1, one launch (start us, length us, event | category | flops | bytes accessed | tf_op | source)
XLA Modules:
  0.0 160.2 jit_solution(6932187454266909194)
XLA Ops:
  0.0 3.2 %abs_reduce_fusion.2 = f32[131072]{0:T(1024)S(1)} fusion(f32[2,262144]{1,0:T(2,128)} %param.3, pred[]{:T(512)S(6)} %eq.110), kind=kLoop, calls=%fused_computation.64 | loop fusion | flops 655360 | bytes 2621441 | tf_op jit(solution)/shard_map/reduce_max | solution.py:35
  4.0 0.8 copy-done
  4.8 1.6 divide_convert_fusion
  6.4 9.6 %collective-permute-start = (bf16[2,131072]{1,0:T(2,128)(2,1)}, bf16[2,131072]{1,0:T(2,128)(2,1)}, u32[]{:S(2)}, u32[]{:S(2)}) collective-permute-start(bf16[2,131072]{1,0:T(2,128)(2,1)} %divide_convert_fusion), channel_id=1, source_target_pairs={{0,256},{256,0},{8,264},{264,8},{16,272},{272,16},{24,280},{280,24... | collective-permute-start | bytes 1572872 | tf_op jit(solution)/shard_map/ppermute | solution.py:16
  16.0 2.1 %collective-permute-start.1 = (bf16[512]{0:T(512)(128)(2,1)S(1)}, bf16[512]{0:T(512)(128)(2,1)S(1)}, u32[]{:S(2)}, u32[]{:S(2)}) collective-permute-start(bf16[512]{0:T(512)(128)(2,1)S(1)} %get-tuple-element.17), channel_id=1, source_target_pairs={{0,256},{256,0},{8,264},{264,8},{16,272},{272,16},{24,280},{280,24... | collective-permute-start | bytes 3080 | tf_op jit(solution)/shard_map/ppermute | solution.py:16
  18.2 0.7 fusion.46
  18.9 0.7 fusion.52
  20.3 4.3 %shift-left_add_fusion.2 = s32[256]{0:T(256)S(1)} fusion(s32[]{:T(128)} %bitcast.8, s32[]{:T(128)} %bitcast.7, s32[]{:T(128)} %bitcast.6, s32[]{:T(128)} %bitcast.5, s32[]{:T(128)} %bitcast.4, s32[]{:T(128)} %bitcast.3, s32[]{:T(128)} %bitcast.2), kind=kLoop, calls=%fused_computation.124 | loop fusion | flops 6912 | bytes 1052 | tf_op jit(solution)/shard_map/add | solution.py:25
  24.7 0.3 convolution_bitcast_fusion.2
  25.0 0.7 fusion.50
  25.7 4.3 %shift-left_add_fusion.1 = s32[256]{0:T(256)S(1)} fusion(s32[]{:T(128)} %bitcast.25, s32[]{:T(128)} %bitcast.24, s32[]{:T(128)} %bitcast.23, s32[]{:T(128)} %bitcast.22, s32[]{:T(128)} %bitcast.21, s32[]{:T(128)} %bitcast.20, s32[]{:T(128)} %bitcast.19), kind=kLoop, calls=%fused_computation.122 | loop fusion | flops 6912 | bytes 1052 | tf_op jit(solution)/shard_map/add | solution.py:25
  31.0 0.5 convolution_multiply_fusion.2
  31.5 0.5 convolution_multiply_fusion.1
  31.9 4.3 %shift-left_add_fusion = s32[256]{0:T(256)S(1)} fusion(s32[]{:T(128)} %bitcast.42, s32[]{:T(128)} %bitcast.41, s32[]{:T(128)} %bitcast.40, s32[]{:T(128)} %bitcast.39, s32[]{:T(128)} %bitcast.38, s32[]{:T(128)} %bitcast.37, s32[]{:T(128)} %bitcast.36), kind=kLoop, calls=%fused_computation.120 | loop fusion | flops 6912 | bytes 1052 | tf_op jit(solution)/shard_map/add | solution.py:25
  37.0 24.1 %collective-permute-done.1 = bf16[512]{0:T(512)(128)(2,1)S(1)} collective-permute-done((bf16[512]{0:T(512)(128)(2,1)S(1)}, bf16[512]{0:T(512)(128)(2,1)S(1)}, u32[]{:S(2)}, u32[]{:S(2)}) %collective-permute-start.1) | collective-permute-done | bytes 1056 | tf_op jit(solution)/shard_map/ppermute | solution.py:16
  61.5 2.1 %select_bitcast_fusion = (f32[1,2,1024,128]{3,1,2,0:T(2,128)S(1)}, f32[1,2,1024,128]{3,1,2,0:T(2,128)S(1)}) fusion(bf16[2,131072]{1,0:T(2,128)(2,1)} %collective-permute-done, pred[]{:T(512)S(6)} %eq.110, f32[131072]{0:T(1024)S(1)} %bitcast.212, f32[2,262144]{1,0:T(2,128)S(1)} %copy-done), kind=kLoop, calls=%fused_computation.61 | loop fusion | flops 1310720 | bytes 5242881
  63.8 1.1 fusion.17
  64.9 1.1 fusion.18
  66.0 1.1 fusion.4
  67.1 1.1 fusion.5
  68.2 1.1 abs_reduce_fusion.1
  69.3 1.5 copy.9
  71.7 1.9 %fusion.15 = bf16[2,131072]{1,0:T(2,128)(2,1)} fusion(f32[1,2,1024,128]{3,2,1,0:T(8,128)S(1)} %bitcast.204, f32[131072]{0:T(1024)S(1)} %bitcast.209), kind=kLoop, calls=%fused_computation.65 | loop fusion | flops 524288 | bytes 2097152 | tf_op jit(solution)/shard_map/convert_element_type | solution.py:37
  73.6 3.8 %collective-permute-start.2 = (bf16[2,131072]{1,0:T(2,128)(2,1)}, bf16[2,131072]{1,0:T(2,128)(2,1)S(1)}, u32[]{:S(2)}, u32[]{:S(2)}) collective-permute-start(bf16[2,131072]{1,0:T(2,128)(2,1)} %fusion.15), channel_id=1, source_target_pairs={{0,8},{8,0},{16,24},{24,16},{32,40},{40,32},{48,56},{56,48},{64,72... | collective-permute-start | bytes 1572872 | tf_op jit(solution)/shard_map/ppermute | solution.py:16
  77.4 1.2 convolution_bitcast_fusion
  78.6 2.1 %collective-permute-start.3 = (bf16[512]{0:T(512)(128)(2,1)S(1)}, bf16[512]{0:T(512)(128)(2,1)S(1)}, u32[]{:S(2)}, u32[]{:S(2)}) collective-permute-start(bf16[512]{0:T(512)(128)(2,1)S(1)} %get-tuple-element.13), channel_id=1, source_target_pairs={{0,8},{8,0},{16,24},{24,16},{32,40},{40,32},{48,56},{56,48},{64,72... | collective-permute-start | bytes 3080 | tf_op jit(solution)/shard_map/ppermute | solution.py:16
  80.8 0.3 copy.8
  81.1 0.5 collective-permute-done.3
  82.1 1.4 fusion.13
  83.7 1.1 fusion.19
  84.8 1.1 fusion.20
  85.8 1.1 fusion.2
  86.9 1.1 fusion.3
  88.2 0.3 copy.11
  89.3 1.9 %fusion.16 = bf16[2,131072]{1,0:T(2,128)(2,1)} fusion(f32[1,2,1024,128]{3,2,1,0:T(8,128)S(1)} %bitcast.203, f32[131072]{0:T(1024)S(1)} %bitcast.210), kind=kLoop, calls=%fused_computation.66 | loop fusion | flops 524288 | bytes 2097152 | tf_op jit(solution)/shard_map/convert_element_type | solution.py:37
  91.2 13.9 %collective-permute-start.4 = (bf16[2,131072]{1,0:T(2,128)(2,1)}, bf16[2,131072]{1,0:T(2,128)(2,1)S(1)}, u32[]{:S(2)}, u32[]{:S(2)}) collective-permute-start(bf16[2,131072]{1,0:T(2,128)(2,1)} %fusion.16), channel_id=1, source_target_pairs={{0,1},{1,0},{2,3},{3,2},{4,5},{5,4},{6,7},{7,6},{8,9},{9,8},{10,11... | collective-permute-start | bytes 1572872 | tf_op jit(solution)/shard_map/ppermute | solution.py:16
  105.2 2.2 %collective-permute-start.5 = (bf16[512]{0:T(512)(128)(2,1)S(1)}, bf16[512]{0:T(512)(128)(2,1)S(1)}, u32[]{:S(2)}, u32[]{:S(2)}) collective-permute-start(bf16[512]{0:T(512)(128)(2,1)S(1)} %get-tuple-element.9), channel_id=1, source_target_pairs={{0,1},{1,0},{2,3},{3,2},{4,5},{5,4},{6,7},{7,6},{8,9},{9,8},{10,11... | collective-permute-start | bytes 3080 | tf_op jit(solution)/shard_map/ppermute | solution.py:16
  107.4 0.5 convolution_multiply_fusion
  107.9 0.3 copy.10
  108.2 37.1 %collective-permute-done.5 = bf16[512]{0:T(512)(128)(2,1)S(1)} collective-permute-done((bf16[512]{0:T(512)(128)(2,1)S(1)}, bf16[512]{0:T(512)(128)(2,1)S(1)}, u32[]{:S(2)}, u32[]{:S(2)}) %collective-permute-start.5) | collective-permute-done | bytes 1056 | tf_op jit(solution)/shard_map/ppermute | solution.py:16
  145.8 1.4 fusion.11
  147.4 1.0 fusion.22
  148.4 1.0 fusion.21
  149.4 1.0 fusion.1
  150.5 1.0 fusion
  151.7 0.8 copy.48
  152.5 0.8 copy.49
  153.3 6.9 %pad_maximum_fusion = f32[2,262144]{1,0:T(2,128)} fusion(f32[2,131072]{1,0:T(2,128)S(1)} %bitcast.205, f32[2,131072]{1,0:T(2,128)S(1)} %bitcast.206), kind=kLoop, calls=%fused_computation.6 | loop fusion | flops 524288 | bytes 4194304 | tf_op jit(solution)/shard_map/concatenate | solution.py:74
  (47 shorter events, 4.8 us)
Async XLA Ops:
  3.2 1.6 copy-start
  3.7 14.4 %copy-start.2 = (s32[3,7]{1,0:T(4,128)S(1)}, s32[3,7]{1,0:T(4,128)}, u32[]{:S(2)}) copy-start(s32[3,7]{1,0:T(4,128)} %param.5) | copy-start | bytes 256
  3.7 20.9 %copy-start.1 = (f32[3,2,128,128]{3,2,1,0:T(8,128)S(1)}, f32[3,2,128,128]{3,2,1,0:T(8,128)}, u32[]{:S(2)}) copy-start(f32[3,2,128,128]{3,2,1,0:T(8,128)} %param.4) | copy-start | bytes 1179652
  6.4 55.1 %collective-permute-start = (bf16[2,131072]{1,0:T(2,128)(2,1)}, bf16[2,131072]{1,0:T(2,128)(2,1)}, u32[]{:S(2)}, u32[]{:S(2)}) collective-permute-start(bf16[2,131072]{1,0:T(2,128)(2,1)} %divide_convert_fusion), channel_id=1, source_target_pairs={{0,256},{256,0},{8,264},{264,8},{16,272},{272,16},{24,280},{280,24... | collective-permute-start | bytes 1572872 | tf_op jit(solution)/shard_map/ppermute | solution.py:16
  16.0 45.1 %collective-permute-start.1 = (bf16[512]{0:T(512)(128)(2,1)S(1)}, bf16[512]{0:T(512)(128)(2,1)S(1)}, u32[]{:S(2)}, u32[]{:S(2)}) collective-permute-start(bf16[512]{0:T(512)(128)(2,1)S(1)} %get-tuple-element.17), channel_id=1, source_target_pairs={{0,256},{256,0},{8,264},{264,8},{16,272},{272,16},{24,280},{280,24... | collective-permute-start | bytes 3080 | tf_op jit(solution)/shard_map/ppermute | solution.py:16
  73.6 8.5 %collective-permute-start.2 = (bf16[2,131072]{1,0:T(2,128)(2,1)}, bf16[2,131072]{1,0:T(2,128)(2,1)S(1)}, u32[]{:S(2)}, u32[]{:S(2)}) collective-permute-start(bf16[2,131072]{1,0:T(2,128)(2,1)} %fusion.15), channel_id=1, source_target_pairs={{0,8},{8,0},{16,24},{24,16},{32,40},{40,32},{48,56},{56,48},{64,72... | collective-permute-start | bytes 1572872 | tf_op jit(solution)/shard_map/ppermute | solution.py:16
  78.6 3.0 %collective-permute-start.3 = (bf16[512]{0:T(512)(128)(2,1)S(1)}, bf16[512]{0:T(512)(128)(2,1)S(1)}, u32[]{:S(2)}, u32[]{:S(2)}) collective-permute-start(bf16[512]{0:T(512)(128)(2,1)S(1)} %get-tuple-element.13), channel_id=1, source_target_pairs={{0,8},{8,0},{16,24},{24,16},{32,40},{40,32},{48,56},{56,48},{64,72... | collective-permute-start | bytes 3080 | tf_op jit(solution)/shard_map/ppermute | solution.py:16
  91.2 54.5 %collective-permute-start.4 = (bf16[2,131072]{1,0:T(2,128)(2,1)}, bf16[2,131072]{1,0:T(2,128)(2,1)S(1)}, u32[]{:S(2)}, u32[]{:S(2)}) collective-permute-start(bf16[2,131072]{1,0:T(2,128)(2,1)} %fusion.16), channel_id=1, source_target_pairs={{0,1},{1,0},{2,3},{3,2},{4,5},{5,4},{6,7},{7,6},{8,9},{9,8},{10,11... | collective-permute-start | bytes 1572872 | tf_op jit(solution)/shard_map/ppermute | solution.py:16
  105.2 40.1 %collective-permute-start.5 = (bf16[512]{0:T(512)(128)(2,1)S(1)}, bf16[512]{0:T(512)(128)(2,1)S(1)}, u32[]{:S(2)}, u32[]{:S(2)}) collective-permute-start(bf16[512]{0:T(512)(128)(2,1)S(1)} %get-tuple-element.9), channel_id=1, source_target_pairs={{0,1},{1,0},{2,3},{3,2},{4,5},{5,4},{6,7},{7,6},{8,9},{9,8},{10,11... | collective-permute-start | bytes 3080 | tf_op jit(solution)/shard_map/ppermute | solution.py:16
where the time goes:
time: 161 us; the launch traced here: 160 us
  waiting for transfers between devices  61.8 us (38%)
  other arithmetic  36.4 us (23%)
  starting transfers between devices  33.7 us (21%)
  matrix products  16 us (10%)
  local copies, waits for them, and re-layouts  9.78 us (6%)
  between operations  2.5 us (2%)
    ppermute x6, waiting for transfers between devices, from_partner(): return lax.ppermute(block, axis, route)  61.8 us
    ppermute x6, starting transfers between devices, from_partner(): return lax.ppermute(block, axis, route)  33.7 us
    add x3, other arithmetic, full_gate(): gate_index = gate_index + ((cells >> places[bit_pos] & 1) << bit_pos)  13 us
    concatenate x1, other arithmetic, run_layer(): jnp.concatenate([result[:, :, :128].reshape(2, -1), result[:, :, 128:].re...  6.94 us
    convert_element_type x3, other arithmetic, encode(): (shaped / scales.astype(jnp.float32)[None, :, None]).astype(jnp.bfloat16)  5.31 us
    unnamed x4, other arithmetic  5.14 us
    unnamed x23, local copies, waits for them, and re-layouts  5.09 us
    reduce_max x6, other arithmetic, encode(): magnitude = jnp.max(jnp.abs(shaped), axis=(0, 2)) + 1e-06  4.94 us
  transfers between devices with their start and end apart: 6, of which 3 were waited for; matrix products, arithmetic and copies ran while one was open for 13% of the time, Pallas kernels for 0%

commit v1 on v0

v1 whole, which is shorter than its diff:
```python
import functools

import jax
import jax.numpy as jnp
from jax import lax
from jax.experimental import pallas as pl
from jax.experimental.pallas import tpu as pltpu
from jax.sharding import PartitionSpec as P

LAYERS = 3
ROWS = 1024
CHUNKS = 8
STEP = ROWS // CHUNKS
PAIRS = STEP // 2


def scaled(parts):
    peak = jnp.maximum(
        jnp.maximum(jnp.abs(parts[0]), jnp.abs(parts[1])),
        jnp.maximum(jnp.abs(parts[2]), jnp.abs(parts[3])),
    )
    magnitude = jnp.max(peak, axis=1, keepdims=True) + 1e-06
    scale = magnitude.astype(jnp.bfloat16).astype(jnp.float32)
    inverse = 1.0 / scale
    coded = [(part * inverse).astype(jnp.bfloat16).astype(jnp.float32) for part in parts]
    return [(part * scale).astype(jnp.bfloat16) for part in coded]


def put(ref, chunk, parts):
    ref[chunk, :PAIRS, :128] = parts[0]
    ref[chunk, :PAIRS, 128:] = parts[1]
    ref[chunk, PAIRS:, :128] = parts[2]
    ref[chunk, PAIRS:, 128:] = parts[3]


def quarters(tile):
    return [tile[:PAIRS, :128], tile[:PAIRS, 128:], tile[PAIRS:, :128], tile[PAIRS:, 128:]]


def spread_gate(layer, own, following, gates_ref, sets_ref, weights):
    cells = lax.broadcasted_iota(jnp.int32, (256, 128), 0)
    wanted = lax.broadcasted_iota(jnp.int32, (256, 128), 1)
    cell_in = lax.broadcasted_iota(jnp.int32, (256, 256), 0)
    cell_out = lax.broadcasted_iota(jnp.int32, (256, 256), 1)
    gate_index = jnp.zeros((256, 128), jnp.int32)
    spare = jnp.int32(28)
    for bit_pos in range(7):
        qubit = sets_ref[layer, bit_pos]
        place = jnp.where(qubit == 17, 7, qubit)
        spare = spare - place
        gate_index = gate_index + (((cells >> place) & 1) << bit_pos)
    select = (gate_index == wanted).astype(jnp.float32).astype(jnp.bfloat16)
    same = ((cell_in >> spare) & 1) == ((cell_out >> spare) & 1)
    last_dims = (((1,), (1,)), ((), ()))
    spreads = []
    for part in range(2):
        matrix = gates_ref[layer, part].astype(jnp.bfloat16)
        half_way = lax.dot_general(select, matrix, last_dims, preferred_element_type=jnp.float32)
        whole = lax.dot_general(
            half_way.astype(jnp.bfloat16), select, last_dims, preferred_element_type=jnp.float32
        )
        spreads.append(jnp.where(same, whole, 0.0))
    real, imag = spreads
    for u_in in range(2):
        row = pl.multiple_of(lax.rem(u_in + own + 1, 2) * 256, 256)
        for u_out in range(2):
            if following is None:
                column = u_out * 256
            else:
                column = pl.multiple_of(lax.rem(u_out + following + 1, 2) * 256, 256)
            re = real[u_in * 128 : u_in * 128 + 128, u_out * 128 : u_out * 128 + 128].astype(jnp.bfloat16)
            im = imag[u_in * 128 : u_in * 128 + 128, u_out * 128 : u_out * 128 + 128].astype(jnp.bfloat16)
            weights[layer, pl.ds(row, 128), pl.ds(column, 128)] = re
            weights[layer, pl.ds(row, 128), pl.ds(column + 128, 128)] = im
            weights[layer, pl.ds(row + 128, 128), pl.ds(column, 128)] = -im
            weights[layer, pl.ds(row + 128, 128), pl.ds(column + 128, 128)] = re


def kernel(
    sets_ref,
    gates_ref,
    x_ref,
    out_ref,
    x_v,
    out_v,
    weights,
    send,
    recv,
    kept,
    load_sem,
    rest_sem,
    send_sem,
    recv_sem,
    store_sem,
):
    wide = lax.axis_index("wide")
    narrow = lax.axis_index("narrow")
    n_wide = lax.axis_size("wide")
    own = [wide // (n_wide // 2), lax.rem(wide, 2), narrow]
    partners = [
        {"wide": lax.rem(wide + n_wide // 2, n_wide)},
        {"wide": wide + 1 - 2 * own[1]},
        {"narrow": 1 - narrow},
    ]

    barrier = pltpu.get_barrier_semaphore()
    for partner in partners:
        pl.semaphore_signal(barrier, inc=1, device_id=partner, device_id_type=pl.DeviceIdType.MESH)

    away = pl.multiple_of((1 - own[0]) * 2 * ROWS, 2 * ROWS)
    home = pl.multiple_of(own[0] * 2 * ROWS, 2 * ROWS)

    def load(chunk):
        rows = pl.ds(away + chunk * 2 * STEP, 2 * STEP)
        return pltpu.make_async_copy(x_ref.at[rows], x_v.at[rows], load_sem.at[chunk])

    rest = pltpu.make_async_copy(x_ref.at[pl.ds(home, 2 * ROWS)], x_v.at[pl.ds(home, 2 * ROWS)], rest_sem)

    def exchange(layer, chunk):
        return pltpu.make_async_remote_copy(
            src_ref=send.at[layer, chunk],
            dst_ref=recv.at[layer, chunk],
            send_sem=send_sem.at[layer, chunk],
            recv_sem=recv_sem.at[layer, chunk],
            device_id=partners[layer],
            device_id_type=pl.DeviceIdType.MESH,
        )

    def store(half, chunk):
        rows = pl.ds(pl.multiple_of(half * 2 * ROWS + chunk * 2 * STEP, 2 * STEP), 2 * STEP)
        return pltpu.make_async_copy(out_v.at[rows], out_ref.at[rows], store_sem.at[half, chunk])

    def read(base, chunk):
        start = base + chunk * 2 * STEP
        return [x_v[pl.ds(start + part, PAIRS, stride=4), :] for part in range(4)]

    for chunk in range(CHUNKS):
        load(chunk).start()
    rest.start()

    pl.semaphore_wait(barrier, 3)

    @pl.loop(0, CHUNKS)
    def _(chunk):
        load(chunk).wait()
        put(send.at[0], chunk, scaled(read(away, chunk)))
        exchange(0, chunk).start()

    spread_gate(0, own[0], own[1], gates_ref, sets_ref, weights)
    rest.wait()

    @pl.loop(0, CHUNKS)
    def _(chunk):
        put(kept.at[0], chunk, [part.astype(jnp.bfloat16) for part in read(home, chunk)])

    spread_gate(1, own[1], own[2], gates_ref, sets_ref, weights)
    spread_gate(2, own[2], None, gates_ref, sets_ref, weights)

    def gate(layer, chunk):
        exchange(layer, chunk).wait_recv()
        block = jnp.concatenate([recv[layer, chunk], kept[layer, chunk]], axis=1)
        return jnp.dot(block, weights[layer], preferred_element_type=jnp.float32)

    def advance(layer, chunk):
        result = gate(layer, chunk)
        put(send.at[layer + 1], chunk, scaled(quarters(result[:, :256])))
        exchange(layer + 1, chunk).start()
        kept[layer + 1, chunk] = result[:, 256:].astype(jnp.bfloat16)

    advance(0, 0)

    @pl.loop(1, CHUNKS)
    def _(chunk):
        advance(0, chunk)
        advance(1, chunk - 1)

    advance(1, CHUNKS - 1)

    @pl.loop(0, CHUNKS)
    def _(chunk):
        result = gate(2, chunk)
        for half in range(2):
            start = half * 2 * ROWS + chunk * 2 * STEP
            for part, value in enumerate(quarters(result[:, half * 256 : half * 256 + 256])):
                out_v[pl.ds(start + part, PAIRS, stride=4), :] = value
            store(half, chunk).start()

    @pl.loop(0, CHUNKS)
    def _(chunk):
        for layer in range(LAYERS):
            exchange(layer, chunk).wait_send()
        for half in range(2):
            store(half, chunk).wait()


def on_device(amplitudes, gates, qubit_sets):
    rows = amplitudes.reshape(2, 2 * ROWS, 128).transpose(1, 0, 2).reshape(4 * ROWS, 128)
    out = pl.pallas_call(
        kernel,
        out_shape=jax.ShapeDtypeStruct((4 * ROWS, 128), jnp.float32),
        in_specs=[
            pl.BlockSpec(memory_space=pltpu.SMEM),
            pl.BlockSpec(memory_space=pltpu.VMEM),
            pl.BlockSpec(memory_space=pl.ANY),
        ],
        out_specs=pl.BlockSpec(memory_space=pl.ANY),
        scratch_shapes=[
            pltpu.VMEM((4 * ROWS, 128), jnp.float32),
            pltpu.VMEM((4 * ROWS, 128), jnp.float32),
            pltpu.VMEM((LAYERS, 512, 512), jnp.bfloat16),
            pltpu.VMEM((LAYERS, CHUNKS, STEP, 256), jnp.bfloat16),
            pltpu.VMEM((LAYERS, CHUNKS, STEP, 256), jnp.bfloat16),
            pltpu.VMEM((LAYERS, CHUNKS, STEP, 256), jnp.bfloat16),
            pltpu.SemaphoreType.DMA((CHUNKS,)),
            pltpu.SemaphoreType.DMA,
            pltpu.SemaphoreType.DMA((LAYERS, CHUNKS)),
            pltpu.SemaphoreType.DMA((LAYERS, CHUNKS)),
            pltpu.SemaphoreType.DMA((2, CHUNKS)),
        ],
        compiler_params=pltpu.CompilerParams(
            collective_id=0, has_side_effects=True, vmem_limit_bytes=40 * 1024 * 1024
        ),
        name="layers",
    )(qubit_sets, gates, rows)
    return out.reshape(2 * ROWS, 2, 128).transpose(1, 0, 2).reshape(2, 2 * ROWS * 128)


def solution(mesh):
    in_specs = (P(None, ("wide", "mid", "narrow")), P(), P())
    out_specs = P(None, ("wide", "mid", "narrow"))
    return jax.shard_map(
        on_device, mesh=mesh, in_specs=in_specs, out_specs=out_specs, check_vma=False
    )
```

time: 161 us -> 116 us (0.72)
  Pallas kernels: 0 us -> 111 us
  waiting for transfers between devices: 61.8 us -> 0 us
  other arithmetic: 36.4 us -> 0 us
  starting transfers between devices: 33.7 us -> 0 us
  matrix products: 16 us -> 0 us
  local copies, waits for them, and re-layouts: 9.78 us -> 4.59 us
  between operations: 2.5 us -> 0.01 us
    pallas_call x0 -> x1, Pallas kernels: none -> 111 us  [on_device(): pl.pallas_call(kernel, out_shape=jax.ShapeDtypeStruct((4 * ROWS, 128), jn...]
    ppermute x6 -> x0, waiting for transfers between devices: 61.8 us -> none  [from_partner(): return lax.ppermute(block, axis, route)]
    ppermute x6 -> x0, starting transfers between devices: 33.7 us -> none  [from_partner(): return lax.ppermute(block, axis, route)]
    dot_general x18 -> x0, matrix products: 16 us -> none  [the longest x3 3.3 us: apply_gate(): jnp.einsum('bk,rk->br', block_in[1], matrix[1], precision=lax.Precision.H...]
    add x3 -> x0, other arithmetic: 13 us -> none  [full_gate(): gate_index = gate_index + ((cells >> places[bit_pos] & 1) << bit_pos)]
    concatenate x1 -> x0, other arithmetic: 6.94 us -> none  [run_layer(): jnp.concatenate([result[:, :, :128].reshape(2, -1), result[:, :, 128:].re...]
    convert_element_type x12 -> x0, other arithmetic: 5.64 us -> none  [the longest x3 5.31 us: encode(): (shaped / scales.astype(jnp.float32)[None, :, None]).astype(jnp.bfloat16)]
    unnamed x4 -> x0, other arithmetic: 5.14 us -> none
  transfers between devices with their start and end apart: 6 -> 0, of which waited for: 3 -> 0; matrix products, arithmetic and copies ran while one was open for 13% -> 0% of each run, Pallas kernels for 0% -> 0%
where the time goes in v1:
time: 116 us
  Pallas kernels  111 us (96%)
  local copies, waits for them, and re-layouts  4.59 us (4%)
    pallas_call x1, Pallas kernels, on_device(): pl.pallas_call(kernel, out_shape=jax.ShapeDtypeStruct((4 * ROWS, 128), jn...  111 us
    unnamed x7, local copies, waits for them, and re-layouts  4.59 us

profile of v1, /device:TPU:1, one launch (start us, length us, event | category | flops | bytes accessed | tf_op | source)
XLA Modules:
  0.0 116.0 jit_solution(14124395286520233554)
XLA Ops:
  0.0 0.0 copy-start
  0.0 1.6 %copy-done = f32[2,262144]{1,0:T(2,128)S(1)} copy-done((f32[2,262144]{1,0:T(2,128)S(1)}, f32[2,262144]{1,0:T(2,128)}, u32[]{:S(2)}) %copy-start) | copy-done | bytes 2097176
  1.6 0.0 copy-start.1
  1.6 1.0 copy-done.1
  2.6 0.0 copy-start.2
  2.6 0.7 copy-done.2
  3.3 111.4 %layers.1 = f32[4096,128]{1,0:T(8,128)S(1)} custom-call(s32[3,7]{1,0:T(4,128)S(1)} %copy-done.2, f32[3,2,128,128]{3,2,1,0:T(8,128)S(1)} %copy-done.1, f32[4096,128]{1,0:T(8,128)S(1)} %bitcast.11), custom_call_target="tpu_custom_call" | custom-call | tf_op jit(solution)/shard_map/layers/pallas_call | solution.py:198
  114.6 1.3 %copy.7 = f32[2,262144]{1,0:T(2,128)} copy(f32[2,262144]{1,0:T(2,128)S(1)} %bitcast.10) | data formatting | bytes 4194304
Async XLA Ops:
  0.0 1.6 %copy-start = (f32[2,262144]{1,0:T(2,128)S(1)}, f32[2,262144]{1,0:T(2,128)}, u32[]{:S(2)}) copy-start(f32[2,262144]{1,0:T(2,128)} %param.3) | copy-start | bytes 6291460
  1.6 1.0 copy-start.1
  2.6 0.7 copy-start.2

commit v2 on v1

--- a/solution.py
+++ b/solution.py
@@ -12,6 +12,7 @@
 CHUNKS = 8
 STEP = ROWS // CHUNKS
 PAIRS = STEP // 2
+EARLY = CHUNKS // 2
 
 
 def scaled(parts):
@@ -77,10 +78,12 @@
 
 
 def kernel(
+    sets_hbm,
+    gates_hbm,
+    x_ref,
+    out_ref,
     sets_ref,
     gates_ref,
-    x_ref,
-    out_ref,
     x_v,
     out_v,
     weights,
@@ -97,14 +100,13 @@
     narrow = lax.axis_index("narrow")
     n_wide = lax.axis_size("wide")
     own = [wide // (n_wide // 2), lax.rem(wide, 2), narrow]
-    partners = [
-        {"wide": lax.rem(wide + n_wide // 2, n_wide)},
-        {"wide": wide + 1 - 2 * own[1]},
-        {"narrow": 1 - narrow},
-    ]
+    across = lax.rem(wide + n_wide // 2, n_wide)
+    partner_f = {"wide": across}
+    partner_g = {"wide": across, "narrow": 1 - narrow}
+    core = {"wide": wide + 1 - 2 * own[1]}
 
     barrier = pltpu.get_barrier_semaphore()
-    for partner in partners:
+    for partner in (partner_f, partner_g, core):
         pl.semaphore_signal(barrier, inc=1, device_id=partner, device_id_type=pl.DeviceIdType.MESH)
 
     away = pl.multiple_of((1 - own[0]) * 2 * ROWS, 2 * ROWS)
@@ -114,15 +116,20 @@
         rows = pl.ds(away + chunk * 2 * STEP, 2 * STEP)
         return pltpu.make_async_copy(x_ref.at[rows], x_v.at[rows], load_sem.at[chunk])
 
-    rest = pltpu.make_async_copy(x_ref.at[pl.ds(home, 2 * ROWS)], x_v.at[pl.ds(home, 2 * ROWS)], rest_sem)
-
-    def exchange(layer, chunk):
+    rest = [
+        pltpu.make_async_copy(x_ref.at[pl.ds(home, 2 * ROWS)], x_v.at[pl.ds(home, 2 * ROWS)], rest_sem.at[0]),
+        pltpu.make_async_copy(gates_hbm, gates_ref, rest_sem.at[1]),
+        pltpu.make_async_copy(sets_hbm, sets_ref, rest_sem.at[2]),
+    ]
+
+    def exchange(stage, chunk, partner):
+        source = send.at[stage, chunk] if stage < 3 else recv.at[2, chunk]
         return pltpu.make_async_remote_copy(
-            src_ref=send.at[layer, chunk],
-            dst_ref=recv.at[layer, chunk],
-            send_sem=send_sem.at[layer, chunk],
-            recv_sem=recv_sem.at[layer, chunk],
-            device_id=partners[layer],
+            src_ref=source,
+            dst_ref=recv.at[stage, chunk],
+            send_sem=send_sem.at[stage, chunk],
+            recv_sem=recv_sem.at[stage, chunk],
+            device_id=partner,
             device_id_type=pl.DeviceIdType.MESH,
         )
 
@@ -136,18 +143,25 @@
 
     for chunk in range(CHUNKS):
         load(chunk).start()
-    rest.start()
-
-    pl.semaphore_wait(barrier, 3)
-
-    @pl.loop(0, CHUNKS)
-    def _(chunk):
+    for copy in rest:
+        copy.start()
+
+    def first(chunk):
         load(chunk).wait()
         put(send.at[0], chunk, scaled(read(away, chunk)))
-        exchange(0, chunk).start()
-
+
+    first(0)
+    pl.semaphore_wait(barrier, 3)
+    exchange(0, 0, partner_f).start()
+
+    @pl.loop(1, CHUNKS)
+    def _(chunk):
+        first(chunk)
+        exchange(0, chunk, partner_f).start()
+
+    for copy in rest:
+        copy.wait()
     spread_gate(0, own[0], own[1], gates_ref, sets_ref, weights)
-    rest.wait()
 
     @pl.loop(0, CHUNKS)
     def _(chunk):
@@ -156,29 +170,44 @@
     spread_gate(1, own[1], own[2], gates_ref, sets_ref, weights)
     spread_gate(2, own[2], None, gates_ref, sets_ref, weights)
 
-    def gate(layer, chunk):
-        exchange(layer, chunk).wait_recv()
-        block = jnp.concatenate([recv[layer, chunk], kept[layer, chunk]], axis=1)
+    def gate(layer, stage, chunk):
+        exchange(stage, chunk, core).wait_recv()
+        block = jnp.concatenate([recv[stage, chunk], kept[layer, chunk]], axis=1)
         return jnp.dot(block, weights[layer], preferred_element_type=jnp.float32)
 
-    def advance(layer, chunk):
-        result = gate(layer, chunk)
+    def advance(layer, chunk, partner):
+        result = gate(layer, layer, chunk)
         put(send.at[layer + 1], chunk, scaled(quarters(result[:, :256])))
-        exchange(layer + 1, chunk).start()
+        exchange(layer + 1, chunk, partner).start()
         kept[layer + 1, chunk] = result[:, 256:].astype(jnp.bfloat16)
 
-    advance(0, 0)
-
-    @pl.loop(1, CHUNKS)
-    def _(chunk):
-        advance(0, chunk)
-        advance(1, chunk - 1)
-
-    advance(1, CHUNKS - 1)
+    advance(0, 0, core)
+
+    @pl.loop(1, EARLY + 1)
+    def _(chunk):
+        advance(0, chunk, core)
+        advance(1, chunk - 1, partner_g)
+
+    @pl.loop(EARLY + 1, CHUNKS)
+    def _(chunk):
+        advance(0, chunk, core)
+        advance(1, chunk - 1, partner_f)
+
+    advance(1, CHUNKS - 1, partner_f)
+
+    @pl.loop(0, EARLY)
+    def _(chunk):
+        exchange(2, chunk, core).wait_recv()
+        exchange(3, chunk, partner_f).start()
+
+    @pl.loop(EARLY, CHUNKS)
+    def _(chunk):
+        exchange(2, chunk, core).wait_recv()
+        exchange(3, chunk, partner_g).start()
 
     @pl.loop(0, CHUNKS)
     def _(chunk):
-        result = gate(2, chunk)
+        result = gate(2, 3, chunk)
         for half in range(2):
             start = half * 2 * ROWS + chunk * 2 * STEP
             for part, value in enumerate(quarters(result[:, half * 256 : half * 256 + 256])):
@@ -187,8 +216,8 @@
 
     @pl.loop(0, CHUNKS)
     def _(chunk):
-        for layer in range(LAYERS):
-            exchange(layer, chunk).wait_send()
+        for stage in range(4):
+            exchange(stage, chunk, core).wait_send()
         for half in range(2):
             store(half, chunk).wait()
 
@@ -199,26 +228,28 @@
         kernel,
         out_shape=jax.ShapeDtypeStruct((4 * ROWS, 128), jnp.float32),
         in_specs=[
-            pl.BlockSpec(memory_space=pltpu.SMEM),
-            pl.BlockSpec(memory_space=pltpu.VMEM),
+            pl.BlockSpec(memory_space=pl.ANY),
+            pl.BlockSpec(memory_space=pl.ANY),
             pl.BlockSpec(memory_space=pl.ANY),
         ],
         out_specs=pl.BlockSpec(memory_space=pl.ANY),
         scratch_shapes=[
+            pltpu.SMEM((LAYERS, 7), jnp.int32),
+            pltpu.VMEM((LAYERS, 2, 128, 128), jnp.float32),
             pltpu.VMEM((4 * ROWS, 128), jnp.float32),
             pltpu.VMEM((4 * ROWS, 128), jnp.float32),
             pltpu.VMEM((LAYERS, 512, 512), jnp.bfloat16),
-            pltpu.VMEM((LAYERS, CHUNKS, STEP, 256), jnp.bfloat16),
-            pltpu.VMEM((LAYERS, CHUNKS, STEP, 256), jnp.bfloat16),
-            pltpu.VMEM((LAYERS, CHUNKS, STEP, 256), jnp.bfloat16),
+            pltpu.VMEM((3, CHUNKS, STEP, 256), jnp.bfloat16),
+            pltpu.VMEM((4, CHUNKS, STEP, 256), jnp.bfloat16),
+            pltpu.VMEM((3, CHUNKS, STEP, 256), jnp.bfloat16),
             pltpu.SemaphoreType.DMA((CHUNKS,)),
-            pltpu.SemaphoreType.DMA,
-            pltpu.SemaphoreType.DMA((LAYERS, CHUNKS)),
-            pltpu.SemaphoreType.DMA((LAYERS, CHUNKS)),
+            pltpu.SemaphoreType.DMA((3,)),
+            pltpu.SemaphoreType.DMA((4, CHUNKS)),
+            pltpu.SemaphoreType.DMA((4, CHUNKS)),
             pltpu.SemaphoreType.DMA((2, CHUNKS)),
         ],
         compiler_params=pltpu.CompilerParams(
-            collective_id=0, has_side_effects=True, vmem_limit_bytes=40 * 1024 * 1024
+            collective_id=0, has_side_effects=True, vmem_limit_bytes=60 * 1024 * 1024
         ),
         name="layers",
     )(qubit_sets, gates, rows)

time: 116 us -> 112 us (0.966)
  Pallas kernels: 111 us -> 109 us
  local copies, waits for them, and re-layouts: 4.59 us -> 2.61 us
    pallas_call x1, Pallas kernels: 111 us -> 109 us  [on_device(): pl.pallas_call(kernel, out_shape=jax.ShapeDtypeStruct((4 * ROWS, 128), jn...]
    unnamed x7 -> x1, local copies, waits for them, and re-layouts: 4.59 us -> 2.61 us
where the time goes in v2:
time: 112 us; the launch traced here: 111 us
  Pallas kernels  109 us (97%)
  local copies, waits for them, and re-layouts  2.61 us (2%)
    pallas_call x1, Pallas kernels, on_device(): pl.pallas_call(kernel, out_shape=jax.ShapeDtypeStruct((4 * ROWS, 128), jn...  109 us
    unnamed x1, local copies, waits for them, and re-layouts  2.61 us

profile of v2, /device:TPU:1, one launch (start us, length us, event | category | flops | bytes accessed | tf_op | source)
XLA Modules:
  0.0 111.4 jit_solution(4476543304854249709)
XLA Ops:
  0.0 108.7 %layers.1 = f32[4096,128]{1,0:T(8,128)} custom-call(s32[3,7]{1,0:T(4,128)} %sets_hbm.1, f32[3,2,128,128]{3,2,1,0:T(8,128)} %gates_hbm.1, f32[4096,128]{1,0:T(8,128)} %bitcast.11), custom_call_target="tpu_custom_call" | custom-call | tf_op jit(solution)/shard_map/layers/pallas_call | solution.py:227
  108.8 2.6 %copy.7 = f32[2,262144]{1,0:T(2,128)} copy(f32[2,262144]{1,0:T(2,128)} %bitcast.10) | data formatting | bytes 4194304

commit v3 on v2

--- a/solution.py
+++ b/solution.py
@@ -146,42 +146,49 @@
     for copy in rest:
         copy.start()
 
-    def first(chunk):
-        load(chunk).wait()
-        put(send.at[0], chunk, scaled(read(away, chunk)))
-
-    first(0)
+    def send_first():
+        @pl.loop(0, CHUNKS)
+        def _(chunk):
+            load(chunk).wait()
+            put(send.at[0], chunk, scaled(read(away, chunk)))
+            exchange(0, chunk, partner_f).start()
+
+    def prepare():
+        for copy in rest:
+            copy.wait()
+        spread_gate(0, own[0], own[1], gates_ref, sets_ref, weights)
+
+        @pl.loop(0, CHUNKS)
+        def _(chunk):
+            put(kept.at[0], chunk, [part.astype(jnp.bfloat16) for part in read(home, chunk)])
+
+        spread_gate(1, own[1], own[2], gates_ref, sets_ref, weights)
+        spread_gate(2, own[2], None, gates_ref, sets_ref, weights)
+        exchange(0, 0, core).wait_recv()
+
     pl.semaphore_wait(barrier, 3)
-    exchange(0, 0, partner_f).start()
-
-    @pl.loop(1, CHUNKS)
-    def _(chunk):
-        first(chunk)
-        exchange(0, chunk, partner_f).start()
-
-    for copy in rest:
-        copy.wait()
-    spread_gate(0, own[0], own[1], gates_ref, sets_ref, weights)
-
-    @pl.loop(0, CHUNKS)
-    def _(chunk):
-        put(kept.at[0], chunk, [part.astype(jnp.bfloat16) for part in read(home, chunk)])
-
-    spread_gate(1, own[1], own[2], gates_ref, sets_ref, weights)
-    spread_gate(2, own[2], None, gates_ref, sets_ref, weights)
+    send_first()
+    prepare()
+
+    holds = lax.rem(wide // (n_wide // 8), 8) == 7
+    held = jnp.where(holds, 1, 0)
 
     def gate(layer, stage, chunk):
-        exchange(stage, chunk, core).wait_recv()
         block = jnp.concatenate([recv[stage, chunk], kept[layer, chunk]], axis=1)
         return jnp.dot(block, weights[layer], preferred_element_type=jnp.float32)
 
-    def advance(layer, chunk, partner):
+    def advance(layer, chunk, partner, arrived=False, hold=False):
+        if not arrived:
+            exchange(layer, chunk, core).wait_recv()
         result = gate(layer, layer, chunk)
         put(send.at[layer + 1], chunk, scaled(quarters(result[:, :256])))
-        exchange(layer + 1, chunk, partner).start()
+        if hold:
+            pl.when(jnp.logical_not(holds))(exchange(layer + 1, chunk, partner).start)
+        else:
+            exchange(layer + 1, chunk, partner).start()
         kept[layer + 1, chunk] = result[:, 256:].astype(jnp.bfloat16)
 
-    advance(0, 0, core)
+    advance(0, 0, core, arrived=True)
 
     @pl.loop(1, EARLY + 1)
     def _(chunk):
@@ -191,22 +198,33 @@
     @pl.loop(EARLY + 1, CHUNKS)
     def _(chunk):
         advance(0, chunk, core)
-        advance(1, chunk - 1, partner_f)
-
-    advance(1, CHUNKS - 1, partner_f)
+        advance(1, chunk - 1, partner_f, hold=True)
+
+    advance(1, CHUNKS - 1, partner_f, hold=True)
+
+    def relay(chunk, partner):
+        exchange(2, chunk, core).wait_recv()
+        exchange(3, chunk, partner).start()
+
+    @pl.when(holds)
+    def _():
+        relay(EARLY, partner_g)
+
+        @pl.loop(EARLY, CHUNKS)
+        def _(chunk):
+            exchange(2, chunk, partner_f).start()
 
     @pl.loop(0, EARLY)
     def _(chunk):
-        exchange(2, chunk, core).wait_recv()
-        exchange(3, chunk, partner_f).start()
-
-    @pl.loop(EARLY, CHUNKS)
-    def _(chunk):
-        exchange(2, chunk, core).wait_recv()
-        exchange(3, chunk, partner_g).start()
+        relay(chunk, partner_f)
+
+    @pl.loop(EARLY + held, CHUNKS)
+    def _(chunk):
+        relay(chunk, partner_g)
 
     @pl.loop(0, CHUNKS)
     def _(chunk):
+        exchange(3, chunk, core).wait_recv()
         result = gate(2, 3, chunk)
         for half in range(2):
             start = half * 2 * ROWS + chunk * 2 * STEP

time: 112 us -> 109 us (0.973)
  the two profiles are of different devices: /device:TPU:1 before, /device:TPU:121 now
where the time goes in v3:
time: 109 us
  Pallas kernels  106 us (97%)
  local copies, waits for them, and re-layouts  2.61 us (2%)
    pallas_call x1, Pallas kernels, on_device(): pl.pallas_call(kernel, out_shape=jax.ShapeDtypeStruct((4 * ROWS, 128), jn...  106 us
    unnamed x1, local copies, waits for them, and re-layouts  2.61 us

profile of v3, /device:TPU:121, one launch (start us, length us, event | category | flops | bytes accessed | tf_op | source)
XLA Modules:
  0.0 108.5 jit_solution(431327557640056372)
XLA Ops:
  0.0 105.9 %layers.1 = f32[4096,128]{1,0:T(8,128)} custom-call(s32[3,7]{1,0:T(4,128)} %sets_hbm.1, f32[3,2,128,128]{3,2,1,0:T(8,128)} %gates_hbm.1, f32[4096,128]{1,0:T(8,128)} %bitcast.11), custom_call_target="tpu_custom_call" | custom-call | tf_op jit(solution)/shard_map/layers/pallas_call | solution.py:245
  105.9 2.6 %copy.7 = f32[2,262144]{1,0:T(2,128)} copy(f32[2,262144]{1,0:T(2,128)} %bitcast.10) | data formatting | bytes 4194304

commit v4 on v3

--- a/solution.py
+++ b/solution.py
@@ -85,7 +85,6 @@
     sets_ref,
     gates_ref,
     x_v,
-    out_v,
     weights,
     send,
     recv,
@@ -94,7 +93,7 @@
     rest_sem,
     send_sem,
     recv_sem,
-    store_sem,
+    ready_sem,
 ):
     wide = lax.axis_index("wide")
     narrow = lax.axis_index("narrow")
@@ -106,8 +105,18 @@
     core = {"wide": wide + 1 - 2 * own[1]}
 
     barrier = pltpu.get_barrier_semaphore()
-    for partner in (partner_f, partner_g, core):
-        pl.semaphore_signal(barrier, inc=1, device_id=partner, device_id_type=pl.DeviceIdType.MESH)
+    lower = narrow == 0
+
+    def greet(semaphore, partner):
+        pl.semaphore_signal(semaphore, inc=1, device_id=partner, device_id_type=pl.DeviceIdType.MESH)
+
+    greet(barrier, partner_f)
+    greet(barrier, core)
+
+    @pl.when(lower)
+    def _():
+        greet(barrier, partner_g)
+
 
     away = pl.multiple_of((1 - own[0]) * 2 * ROWS, 2 * ROWS)
     home = pl.multiple_of(own[0] * 2 * ROWS, 2 * ROWS)
@@ -133,10 +142,6 @@
             device_id_type=pl.DeviceIdType.MESH,
         )
 
-    def store(half, chunk):
-        rows = pl.ds(pl.multiple_of(half * 2 * ROWS + chunk * 2 * STEP, 2 * STEP), 2 * STEP)
-        return pltpu.make_async_copy(out_v.at[rows], out_ref.at[rows], store_sem.at[half, chunk])
-
     def read(base, chunk):
         start = base + chunk * 2 * STEP
         return [x_v[pl.ds(start + part, PAIRS, stride=4), :] for part in range(4)]
@@ -146,11 +151,16 @@
     for copy in rest:
         copy.start()
 
+    def first(chunk):
+        load(chunk).wait()
+        put(send.at[0], chunk, scaled(read(away, chunk)))
+
     def send_first():
-        @pl.loop(0, CHUNKS)
+        exchange(0, 0, partner_f).start()
+
+        @pl.loop(1, CHUNKS)
         def _(chunk):
-            load(chunk).wait()
-            put(send.at[0], chunk, scaled(read(away, chunk)))
+            first(chunk)
             exchange(0, chunk, partner_f).start()
 
     def prepare():
@@ -166,9 +176,22 @@
         spread_gate(2, own[2], None, gates_ref, sets_ref, weights)
         exchange(0, 0, core).wait_recv()
 
-    pl.semaphore_wait(barrier, 3)
+    first(0)
+    @pl.when(lower)
+    def _():
+        pl.semaphore_wait(barrier, 2)
+
+    @pl.when(jnp.logical_not(lower))
+    def _():
+        pl.semaphore_wait(barrier, 3)
+        greet(ready_sem, partner_g)
+
     send_first()
     prepare()
+
+    @pl.when(lower)
+    def _():
+        pl.semaphore_wait(ready_sem, 1)
 
     holds = lax.rem(wide // (n_wide // 8), 8) == 7
     held = jnp.where(holds, 1, 0)
@@ -183,7 +206,7 @@
         result = gate(layer, layer, chunk)
         put(send.at[layer + 1], chunk, scaled(quarters(result[:, :256])))
         if hold:
-            pl.when(jnp.logical_not(holds))(exchange(layer + 1, chunk, partner).start)
+            pl.when(jnp.logical_or(jnp.logical_not(holds), chunk < EARLY + 1))(exchange(layer + 1, chunk, partner).start)
         else:
             exchange(layer + 1, chunk, partner).start()
         kept[layer + 1, chunk] = result[:, 256:].astype(jnp.bfloat16)
@@ -210,7 +233,7 @@
     def _():
         relay(EARLY, partner_g)
 
-        @pl.loop(EARLY, CHUNKS)
+        @pl.loop(EARLY + 1, CHUNKS)
         def _(chunk):
             exchange(2, chunk, partner_f).start()
 
@@ -229,32 +252,28 @@
         for half in range(2):
             start = half * 2 * ROWS + chunk * 2 * STEP
             for part, value in enumerate(quarters(result[:, half * 256 : half * 256 + 256])):
-                out_v[pl.ds(start + part, PAIRS, stride=4), :] = value
-            store(half, chunk).start()
+                out_ref[pl.ds(start + part, PAIRS, stride=4), :] = value
 
     @pl.loop(0, CHUNKS)
     def _(chunk):
         for stage in range(4):
             exchange(stage, chunk, core).wait_send()
-        for half in range(2):
-            store(half, chunk).wait()
 
 
 def on_device(amplitudes, gates, qubit_sets):
     rows = amplitudes.reshape(2, 2 * ROWS, 128).transpose(1, 0, 2).reshape(4 * ROWS, 128)
     out = pl.pallas_call(
         kernel,
-        out_shape=jax.ShapeDtypeStruct((4 * ROWS, 128), jnp.float32),
+        out_shape=pltpu.VMEM((4 * ROWS, 128), jnp.float32),
         in_specs=[
             pl.BlockSpec(memory_space=pl.ANY),
             pl.BlockSpec(memory_space=pl.ANY),
             pl.BlockSpec(memory_space=pl.ANY),
         ],
-        out_specs=pl.BlockSpec(memory_space=pl.ANY),
+        out_specs=pl.BlockSpec(memory_space=pltpu.VMEM),
         scratch_shapes=[
             pltpu.SMEM((LAYERS, 7), jnp.int32),
             pltpu.VMEM((LAYERS, 2, 128, 128), jnp.float32),
-            pltpu.VMEM((4 * ROWS, 128), jnp.float32),
             pltpu.VMEM((4 * ROWS, 128), jnp.float32),
             pltpu.VMEM((LAYERS, 512, 512), jnp.bfloat16),
             pltpu.VMEM((3, CHUNKS, STEP, 256), jnp.bfloat16),
@@ -264,7 +283,7 @@
             pltpu.SemaphoreType.DMA((3,)),
             pltpu.SemaphoreType.DMA((4, CHUNKS)),
             pltpu.SemaphoreType.DMA((4, CHUNKS)),
-            pltpu.SemaphoreType.DMA((2, CHUNKS)),
+            pltpu.SemaphoreType.REGULAR,
         ],
         compiler_params=pltpu.CompilerParams(
             collective_id=0, has_side_effects=True, vmem_limit_bytes=60 * 1024 * 1024

time: 109 us -> 105 us (0.963)
  the two profiles are of different devices: /device:TPU:121 before, /device:TPU:1 now
where the time goes in v4:
time: 105 us; the launch traced here: 104 us
  Pallas kernels  103 us (98%)
  local copies, waits for them, and re-layouts  1.32 us (1%)
    pallas_call x1, Pallas kernels, on_device(): pl.pallas_call(kernel, out_shape=pltpu.VMEM((4 * ROWS, 128), jnp.float32)...  103 us

profile of v4, /device:TPU:1, one launch (start us, length us, event | category | flops | bytes accessed | tf_op | source)
XLA Modules:
  0.0 104.4 jit_solution(979633148822156071)
XLA Ops:
  0.0 103.1 %layers.1 = f32[4096,128]{1,0:T(8,128)S(1)} custom-call(s32[3,7]{1,0:T(4,128)} %sets_hbm.1, f32[3,2,128,128]{3,2,1,0:T(8,128)} %gates_hbm.1, f32[4096,128]{1,0:T(8,128)} %bitcast.11), custom_call_target="tpu_custom_call" | custom-call | tf_op jit(solution)/shard_map/layers/pallas_call | solution.py:265
  103.1 1.3 %copy.7 = f32[2,262144]{1,0:T(2,128)} copy(f32[2,262144]{1,0:T(2,128)S(1)} %bitcast.10) | data formatting | bytes 4194304

commit v5 on v4

--- a/solution.py
+++ b/solution.py
@@ -117,7 +117,6 @@
     def _():
         greet(barrier, partner_g)
 
-
     away = pl.multiple_of((1 - own[0]) * 2 * ROWS, 2 * ROWS)
     home = pl.multiple_of(own[0] * 2 * ROWS, 2 * ROWS)
 
@@ -132,12 +131,13 @@
     ]
 
     def exchange(stage, chunk, partner):
-        source = send.at[stage, chunk] if stage < 3 else recv.at[2, chunk]
+        source = [send.at[0], send.at[1], send.at[2], recv.at[2], send.at[2], recv.at[4]][stage]
+        target = [0, 1, 2, 3, 4, 3][stage]
         return pltpu.make_async_remote_copy(
-            src_ref=source,
-            dst_ref=recv.at[stage, chunk],
-            send_sem=send_sem.at[stage, chunk],
-            recv_sem=recv_sem.at[stage, chunk],
+            src_ref=source.at[chunk],
+            dst_ref=recv.at[target, chunk],
+            send_sem=send_sem.at[[0, 1, 2, 3, 2, 4][stage], chunk],
+            recv_sem=recv_sem.at[target, chunk],
             device_id=partner,
             device_id_type=pl.DeviceIdType.MESH,
         )
@@ -146,10 +146,7 @@
         start = base + chunk * 2 * STEP
         return [x_v[pl.ds(start + part, PAIRS, stride=4), :] for part in range(4)]
 
-    for chunk in range(CHUNKS):
-        load(chunk).start()
-    for copy in rest:
-        copy.start()
+    load(0).start()
 
     def first(chunk):
         load(chunk).wait()
@@ -177,6 +174,12 @@
         exchange(0, 0, core).wait_recv()
 
     first(0)
+
+    for chunk in range(1, CHUNKS):
+        load(chunk).start()
+    for copy in rest:
+        copy.start()
+
     @pl.when(lower)
     def _():
         pl.semaphore_wait(barrier, 2)
@@ -193,60 +196,68 @@
     def _():
         pl.semaphore_wait(ready_sem, 1)
 
-    holds = lax.rem(wide // (n_wide // 8), 8) == 7
+    z_low = wide // (n_wide // 8)
+    holds = z_low == 7
     held = jnp.where(holds, 1, 0)
+    early_lower = EARLY + jnp.where(lax.rem(z_low, 4) == 3, 1, 0)
+    early = jnp.where(lower, early_lower, EARLY)
+    early_from_g = jnp.where(lower, EARLY, early_lower)
 
     def gate(layer, stage, chunk):
         block = jnp.concatenate([recv[stage, chunk], kept[layer, chunk]], axis=1)
         return jnp.dot(block, weights[layer], preferred_element_type=jnp.float32)
 
-    def advance(layer, chunk, partner, arrived=False, hold=False):
+    def advance(layer, chunk, stage, partner, arrived=False):
         if not arrived:
             exchange(layer, chunk, core).wait_recv()
         result = gate(layer, layer, chunk)
         put(send.at[layer + 1], chunk, scaled(quarters(result[:, :256])))
-        if hold:
-            pl.when(jnp.logical_or(jnp.logical_not(holds), chunk < EARLY + 1))(exchange(layer + 1, chunk, partner).start)
+        if stage == 4:
+            pl.when(jnp.logical_not(holds))(exchange(4, chunk, partner_f).start)
         else:
-            exchange(layer + 1, chunk, partner).start()
+            exchange(stage, chunk, partner).start()
         kept[layer + 1, chunk] = result[:, 256:].astype(jnp.bfloat16)
 
-    advance(0, 0, core, arrived=True)
-
-    @pl.loop(1, EARLY + 1)
-    def _(chunk):
-        advance(0, chunk, core)
-        advance(1, chunk - 1, partner_g)
-
-    @pl.loop(EARLY + 1, CHUNKS)
-    def _(chunk):
-        advance(0, chunk, core)
-        advance(1, chunk - 1, partner_f, hold=True)
-
-    advance(1, CHUNKS - 1, partner_f, hold=True)
-
-    def relay(chunk, partner):
+    advance(0, 0, 1, core, arrived=True)
+
+    @pl.loop(1, early + 1)
+    def _(chunk):
+        advance(0, chunk, 1, core)
+        advance(1, chunk - 1, 2, partner_g)
+
+    @pl.loop(early + 1, CHUNKS)
+    def _(chunk):
+        advance(0, chunk, 1, core)
+        advance(1, chunk - 1, 4, partner_f)
+
+    advance(1, CHUNKS - 1, 4, partner_f)
+
+    def relay_to_g(chunk):
+        exchange(4, chunk, core).wait_recv()
+        exchange(5, chunk, partner_g).start()
+
+    @pl.when(holds)
+    def _():
+        relay_to_g(early)
+
+        @pl.loop(early, CHUNKS)
+        def _(chunk):
+            exchange(4, chunk, partner_f).start()
+
+    @pl.loop(0, early_from_g)
+    def _(chunk):
         exchange(2, chunk, core).wait_recv()
-        exchange(3, chunk, partner).start()
-
-    @pl.when(holds)
-    def _():
-        relay(EARLY, partner_g)
-
-        @pl.loop(EARLY + 1, CHUNKS)
-        def _(chunk):
-            exchange(2, chunk, partner_f).start()
-
-    @pl.loop(0, EARLY)
-    def _(chunk):
-        relay(chunk, partner_f)
-
-    @pl.loop(EARLY + held, CHUNKS)
-    def _(chunk):
-        relay(chunk, partner_g)
+        exchange(3, chunk, partner_f).start()
+
+    @pl.loop(early + held, CHUNKS)
+    def _(chunk):
+        relay_to_g(chunk)
+
+    turn_from = jnp.where(z_low == 0, 0, early_from_g)
 
     @pl.loop(0, CHUNKS)
-    def _(chunk):
+    def _(turn):
+        chunk = lax.rem(turn + turn_from, CHUNKS)
         exchange(3, chunk, core).wait_recv()
         result = gate(2, 3, chunk)
         for half in range(2):
@@ -256,8 +267,16 @@
 
     @pl.loop(0, CHUNKS)
     def _(chunk):
-        for stage in range(4):
+        for stage in range(3):
             exchange(stage, chunk, core).wait_send()
+
+    @pl.loop(0, early_from_g)
+    def _(chunk):
+        exchange(3, chunk, core).wait_send()
+
+    @pl.loop(early, CHUNKS)
+    def _(chunk):
+        exchange(5, chunk, core).wait_send()
 
 
 def on_device(amplitudes, gates, qubit_sets):
@@ -277,12 +296,12 @@
             pltpu.VMEM((4 * ROWS, 128), jnp.float32),
             pltpu.VMEM((LAYERS, 512, 512), jnp.bfloat16),
             pltpu.VMEM((3, CHUNKS, STEP, 256), jnp.bfloat16),
-            pltpu.VMEM((4, CHUNKS, STEP, 256), jnp.bfloat16),
+            pltpu.VMEM((5, CHUNKS, STEP, 256), jnp.bfloat16),
             pltpu.VMEM((3, CHUNKS, STEP, 256), jnp.bfloat16),
             pltpu.SemaphoreType.DMA((CHUNKS,)),
             pltpu.SemaphoreType.DMA((3,)),
-            pltpu.SemaphoreType.DMA((4, CHUNKS)),
-            pltpu.SemaphoreType.DMA((4, CHUNKS)),
+            pltpu.SemaphoreType.DMA((5, CHUNKS)),
+            pltpu.SemaphoreType.DMA((5, CHUNKS)),
             pltpu.SemaphoreType.REGULAR,
         ],
         compiler_params=pltpu.CompilerParams(

time: 105 us -> 102 us (0.971)
  Pallas kernels: 103 us -> 101 us
    pallas_call x1, Pallas kernels: 103 us -> 101 us  [on_device(): pl.pallas_call(kernel, out_shape=pltpu.VMEM((4 * ROWS, 128), jnp.float32)...]
where the time goes in v5:
time: 102 us
  Pallas kernels  101 us (99%)
  local copies, waits for them, and re-layouts  1.32 us (1%)
    pallas_call x1, Pallas kernels, on_device(): pl.pallas_call(kernel, out_shape=pltpu.VMEM((4 * ROWS, 128), jnp.float32)...  101 us

profile of v5, /device:TPU:1, one launch (start us, length us, event | category | flops | bytes accessed | tf_op | source)
XLA Modules:
  0.0 102.1 jit_solution(10643056175894045562)
XLA Ops:
  0.0 100.8 %layers.1 = f32[4096,128]{1,0:T(8,128)S(1)} custom-call(s32[3,7]{1,0:T(4,128)} %sets_hbm.1, f32[3,2,128,128]{3,2,1,0:T(8,128)} %gates_hbm.1, f32[4096,128]{1,0:T(8,128)} %bitcast.11), custom_call_target="tpu_custom_call" | custom-call | tf_op jit(solution)/shard_map/layers/pallas_call | solution.py:284
  100.8 1.3 %copy.7 = f32[2,262144]{1,0:T(2,128)} copy(f32[2,262144]{1,0:T(2,128)S(1)} %bitcast.10) | data formatting | bytes 4194304

commit v6 on v5

--- a/solution.py
+++ b/solution.py
@@ -253,7 +253,12 @@
     def _(chunk):
         relay_to_g(chunk)
 
-    turn_from = jnp.where(z_low == 0, 0, early_from_g)
+    @pl.loop(0, CHUNKS)
+    def _(chunk):
+        for stage in range(2):
+            exchange(stage, chunk, core).wait_send()
+
+    turn_from = jnp.where(jnp.logical_and(lower, z_low == 0), 0, early_from_g)
 
     @pl.loop(0, CHUNKS)
     def _(turn):
@@ -267,8 +272,7 @@
 
     @pl.loop(0, CHUNKS)
     def _(chunk):
-        for stage in range(3):
-            exchange(stage, chunk, core).wait_send()
+        exchange(2, chunk, core).wait_send()
 
     @pl.loop(0, early_from_g)
     def _(chunk):

time: 102 us -> 102 us (level)
  no operation moved by 1% of the time
where the time goes in v6:
time: 102 us
  Pallas kernels  101 us (99%)
  local copies, waits for them, and re-layouts  1.32 us (1%)
    pallas_call x1, Pallas kernels, on_device(): pl.pallas_call(kernel, out_shape=pltpu.VMEM((4 * ROWS, 128), jnp.float32)...  101 us

profile of v6, /device:TPU:1, one launch (start us, length us, event | category | flops | bytes accessed | tf_op | source)
XLA Modules:
  0.0 102.1 jit_solution(238758700098576999)
XLA Ops:
  0.0 100.8 %layers.1 = f32[4096,128]{1,0:T(8,128)S(1)} custom-call(s32[3,7]{1,0:T(4,128)} %sets_hbm.1, f32[3,2,128,128]{3,2,1,0:T(8,128)} %gates_hbm.1, f32[4096,128]{1,0:T(8,128)} %bitcast.11), custom_call_target="tpu_custom_call" | custom-call | tf_op jit(solution)/shard_map/layers/pallas_call | solution.py:288
  100.8 1.3 %copy.7 = f32[2,262144]{1,0:T(2,128)} copy(f32[2,262144]{1,0:T(2,128)S(1)} %bitcast.10) | data formatting | bytes 4194304

commit v7 on v6

--- a/solution.py
+++ b/solution.py
@@ -154,6 +154,10 @@
 
     def send_first():
         exchange(0, 0, partner_f).start()
+        for chunk in range(1, CHUNKS):
+            load(chunk).start()
+        for copy in rest:
+            copy.start()
 
         @pl.loop(1, CHUNKS)
         def _(chunk):
@@ -174,11 +178,6 @@
         exchange(0, 0, core).wait_recv()
 
     first(0)
-
-    for chunk in range(1, CHUNKS):
-        load(chunk).start()
-    for copy in rest:
-        copy.start()
 
     @pl.when(lower)
     def _():

time: 102 us -> 104 us (1.020)
    pallas_call x1, Pallas kernels: 101 us -> 102 us  [on_device(): pl.pallas_call(kernel, out_shape=pltpu.VMEM((4 * ROWS, 128), jnp.float32)...]
where the time goes in v7:
time: 104 us; the launch traced here: 103 us
  Pallas kernels  102 us (98%)
  local copies, waits for them, and re-layouts  1.32 us (1%)
    pallas_call x1, Pallas kernels, on_device(): pl.pallas_call(kernel, out_shape=pltpu.VMEM((4 * ROWS, 128), jnp.float32)...  102 us

profile of v7, /device:TPU:1, one launch (start us, length us, event | category | flops | bytes accessed | tf_op | source)
XLA Modules:
  0.0 103.5 jit_solution(2668839318178707507)
XLA Ops:
  0.0 102.1 %layers.1 = f32[4096,128]{1,0:T(8,128)S(1)} custom-call(s32[3,7]{1,0:T(4,128)} %sets_hbm.1, f32[3,2,128,128]{3,2,1,0:T(8,128)} %gates_hbm.1, f32[4096,128]{1,0:T(8,128)} %bitcast.11), custom_call_target="tpu_custom_call" | custom-call | tf_op jit(solution)/shard_map/layers/pallas_call | solution.py:287
  102.2 1.3 %copy.7 = f32[2,262144]{1,0:T(2,128)} copy(f32[2,262144]{1,0:T(2,128)S(1)} %bitcast.10) | data formatting | bytes 4194304
